TPU v7x, 32 devices: a whole 2x2x4 slice. The times are simulated.
32 devices in a mesh: dp: 32 (over z, y, x, core).
Axes of the slice: x: 2, y: 2, z: 4, core: 2. Of those that a mesh axis runs over, the one named last changes fastest.
Arguments:
- gradient: float32 [32, 4096, 128], P('dp'), may hold values from -6 to 6
- residual: float32 [32, 4096, 128], P('dp'), may hold values from -5 to 5
- weights: float32 [4096, 128], replicated, may hold values from -6 to 6
- momentum: float32 [4096, 128], replicated, may hold values from -6 to 6
- sel_idx: int32 [32, 32, 4], replicated, may hold values from 0 to 4095, as said below
- sel_count: int32 [32, 32], replicated, may hold values from 1 to 4, as said below
- gath_idx: int32 [32, 8], replicated, may hold values from 0 to 4095, as said below
- gath_count: int32 [32], replicated, may hold values from 6 to 8, as said below
Outputs:
- new_weights: float32 [4096, 128], replicated
- new_momentum: float32 [4096, 128], replicated
- new_residual: float32 [32, 4096, 128], P('dp')
Inputs may be any that keep to these rules, and one draw needn't show every extreme that they name: Owners' regions are consecutive runs of blocks in owner order covering all 4096 blocks, each of 64 to 192 blocks, some of exactly 192. All 4 entries of sel_idx[s, o] are distinct entries of gath_idx[o], those at or beyond sel_count[s, o] included. `sel_count`: some owner receives exactly 4 used slots from every replica. All 8 entries of gath_idx[o] are distinct blocks of owner o's region. `gath_count`: some owner lists exactly 8 blocks.
All inputs are finite; a program needn't handle non-finite values.
Results may differ from a plain program's by a relative error of at most 0.00002.
Values sent between devices are 32-bit elements; how exact they have to be, the bound alone decides.
A program may use at most 192 MiB of HBM per device.

v0:
```python
import jax
import jax.numpy as jnp
from jax import lax
from jax.sharding import PartitionSpec as P

momentum_coef = 0.9
learning_rate = 0.05


def local(gradient, residual, weights, momentum, sel_idx, sel_count, gath_idx, gath_count):
    my_rank = lax.axis_index("dp")
    accumulated = gradient[0] + residual[0]
    block_count, block_len = accumulated.shape
    capacity = sel_idx.shape[2]
    list_len = gath_idx.shape[1]
    slot_ids = jnp.arange(capacity, dtype=jnp.int32)
    my_ids = lax.dynamic_index_in_dim(sel_idx, my_rank, 0, keepdims=False)
    my_counts = lax.dynamic_index_in_dim(sel_count, my_rank, 0, keepdims=False)
    my_valid = (slot_ids[None, :] < my_counts[:, None]).astype(jnp.float32)
    list_slots = jnp.arange(list_len, dtype=jnp.int32)
    list_valid = (list_slots[None, :] < gath_count[:, None]).astype(jnp.float32)
    listed = (
        jnp.zeros((block_count,), jnp.float32).at[gath_idx.reshape(-1)].max(list_valid.reshape(-1))
    )
    my_mask = (
        jnp.zeros((block_count,), jnp.float32).at[my_ids.reshape(-1)].max(my_valid.reshape(-1))
    )
    blank = jnp.zeros((block_count, block_len), jnp.float32)
    outgoing = accumulated[my_ids] * my_valid[:, :, None]
    incoming = lax.all_to_all(outgoing, "dp", split_axis=0, concat_axis=0, tiled=True)
    owned_ids = lax.dynamic_index_in_dim(sel_idx, my_rank, 1, keepdims=False)
    region = blank.at[owned_ids.reshape(-1)].add(incoming.reshape(-1, block_len))
    out_ids = lax.dynamic_index_in_dim(gath_idx, my_rank, 0, keepdims=False)
    out_valid = lax.dynamic_index_in_dim(list_valid, my_rank, 0, keepdims=False)
    out_values = region[out_ids] * out_valid[:, None]
    flat_lists = gath_idx.reshape(-1)
    update = blank.at[flat_lists].add(lax.all_gather(out_values, "dp", axis=0, tiled=True))
    new_momentum = momentum_coef * momentum + update
    new_weights = weights - learning_rate * new_momentum
    new_residual = (accumulated * (1.0 - my_mask * listed)[:, None])[None]
    return (new_weights, new_momentum, new_residual)


def solution(mesh):
    placed = (P("dp", None, None), P("dp", None, None), P(), P(), P(), P(), P(), P())
    return jax.shard_map(
        local,
        mesh=mesh,
        in_specs=placed,
        out_specs=(P(), P(), P("dp", None, None)),
        check_vma=False,
    )
```

profile of v0, /device:TPU:0, one launch (start us, length us, event | category | flops | bytes accessed | tf_op | source)
XLA Modules:
  0.0 76.6 jit_solution(12751563189343011880)
XLA Ops:
  0.6 0.0 copy-start
  0.6 0.7 copy-done
  1.4 0.7 compare_select_fusion.1
  2.0 0.1 copy.14
  2.1 0.1 reshape.217
  2.3 0.1 fusion.2
  2.3 0.1 reshape.251
  2.4 0.7 fusion.3
  3.2 0.1 reshape.259
  3.3 0.1 copy.15
  3.3 0.1 reshape.212
  3.5 0.8 copy.13
  4.2 0.1 reshape.209
  4.3 1.4 %scatter_custom_fusion.2 = f32[4096]{0:T(1024)S(1)} fusion(s32[128]{0:T(128)S(1)} %fusion.12, f32[128]{0:T(128)S(1)} %reshape.251, f32[]{:T(128)} %constant.14.clone.1), kind=kCustom, calls=%fused_computation.21 | custom fusion | flops 128 | bytes 16388 | tf_op jit(solution)/shard_map/scatter-max | solution.py:26
  5.8 2.3 %scatter_custom_fusion.3 = f32[4096]{0:T(1024)S(1)} fusion(s32[256]{0:T(256)S(1)} %bitcast.23, f32[256]{0:T(256)S(1)} %reshape.259, f32[]{:T(128)} %constant.14.clone.1), kind=kCustom, calls=%fused_computation.19 | custom fusion | flops 256 | bytes 16388 | tf_op jit(solution)/shard_map/scatter-max | solution.py:23
  8.1 0.0 copy-start.3
  8.1 0.0 copy-start.2
  8.1 3.5 %broadcast_multiply_fusion = (f32[1,4096,128]{2,1,0:T(8,128)}, f32[4096,128]{1,0:T(8,128)S(1)}) fusion(f32[4096]{0:T(1024)S(1)} %multiply_subtract_fusion.1, f32[1,4096,128]{2,1,0:T(8,128)} %param.8, f32[1,4096,128]{2,1,0:T(8,128)} %param.9), kind=kLoop, calls=%fused_computation.7 | loop fusion | flops 1048576 | bytes 8404992 | tf_op jit(solution)/shard_map/mul | solution.py:40
  11.6 0.6 gather_fusion
  12.3 0.7 broadcast_multiply_fusion.2
  13.0 7.3 %all-to-all-start = ((f32[32,4,128]{2,1,0:T(4,128)}), f32[32,4,128]{2,1,0:T(4,128)S(1)}, u32[]{:S(2)}, u32[]{:S(2)}) async-start(f32[32,4,128]{2,1,0:T(4,128)} %broadcast_multiply_fusion.2), calls=%async_computation | async-start | bytes 131072 | tf_op jit(solution)/shard_map/all_to_all | solution.py:30
  20.3 0.2 dynamic-slice_reduce_fusion.1
  20.5 0.7 dynamic-slice_reduce_fusion
  21.2 0.1 reshape.210
  21.3 1.8 %broadcast_multiply_fusion.1 = f32[4096,128]{1,0:T(8,128)S(1)} fusion(f32[4096,128]{1,0:T(8,128)} %param.11), kind=kLoop, calls=%fused_computation.10 | loop fusion | flops 524288 | bytes 4194304 | tf_op jit(solution)/shard_map/mul | solution.py:38
  23.1 4.6 %all-to-all-done = f32[32,4,128]{2,1,0:T(4,128)S(1)} async-done(((f32[32,4,128]{2,1,0:T(4,128)}), f32[32,4,128]{2,1,0:T(4,128)S(1)}, u32[]{:S(2)}, u32[]{:S(2)}) %all-to-all-start) | async-done | bytes 65568 | tf_op jit(solution)/shard_map/all_to_all | solution.py:30
  27.7 2.4 %scatter_custom_fusion = f32[4096,128]{1,0:T(8,128)} fusion(s32[128]{0:T(128)S(1)} %fusion.10, f32[128,128]{1,0:T(8,128)S(1)} %bitcast.22, f32[]{:T(128)} %constant.14.clone.1), kind=kCustom, calls=%fused_computation.8 | custom fusion | flops 16384 | bytes 2097156 | tf_op jit(solution)/shard_map/scatter-add | solution.py:32
  30.1 2.1 %gather_fusion.1 = f32[8,128]{1,0:T(8,128)S(1)} fusion(f32[4096,128]{1,0:T(8,128)} %scatter_custom_fusion, s32[1024]{0:T(1024)S(1)} %pad_clamp_fusion), kind=kCustom, calls=%fused_computation.1 | custom fusion | bytes 8224 | tf_op jit(solution)/shard_map/gather | solution.py:35
  32.3 0.1 broadcast_multiply_fusion.3
  32.3 37.7 %all_gather.3 = f32[256,128]{1,0:T(8,128)S(1)} all-gather(f32[8,128]{1,0:T(8,128)S(1)} %broadcast_multiply_fusion.3), channel_id=1, replica_groups=mesh['dp'=32] {'dp'}, dimensions={0}, use_global_device_ids=true | all-gather | bytes 135168 | tf_op jit(solution)/shard_map/all_gather | solution.py:37
  70.0 2.7 %scatter_fusion = f32[4096,128]{1,0:T(8,128)S(1)} fusion(f32[4096,128]{1,0:T(8,128)S(1)} %broadcast_multiply_fusion.1, s32[256]{0:T(256)S(1)} %bitcast.24, f32[256,128]{1,0:T(8,128)S(1)} %all_gather.3), kind=kCustom, calls=%fused_computation.3 | custom fusion | flops 32768 | bytes 394240 | tf_op jit(solution)/shard_map/scatter-add | solution.py:37
  72.7 3.9 %multiply_subtract_fusion = f32[4096,128]{1,0:T(8,128)} fusion(f32[4096,128]{1,0:T(8,128)} %param.10, f32[4096,128]{1,0:T(8,128)S(1)} %scatter_fusion), kind=kLoop, calls=%fused_computation.6 | loop fusion | flops 1048576 | bytes 6291456 | tf_op jit(solution)/shard_map/sub | solution.py:39
  (13 shorter events, 0.1 us)
Async XLA Ops:
  0.6 0.7 copy-start
  8.1 12.2 %copy-start.3 = (s32[32,8]{0,1:T(8,128)S(1)}, s32[32,8]{0,1:T(8,128)}, u32[]{:S(2)}) copy-start(s32[32,8]{0,1:T(8,128)} %param.14) | copy-start | bytes 3076
  8.1 12.4 %copy-start.2 = (s32[32,32,4]{1,2,0:T(4,128)S(1)}, s32[32,32,4]{1,2,0:T(4,128)}, u32[]{:S(2)}) copy-start(s32[32,32,4]{1,2,0:T(4,128)} %param.12) | copy-start | bytes 49156
  13.0 14.7 %all-to-all-start = ((f32[32,4,128]{2,1,0:T(4,128)}), f32[32,4,128]{2,1,0:T(4,128)S(1)}, u32[]{:S(2)}, u32[]{:S(2)}) async-start(f32[32,4,128]{2,1,0:T(4,128)} %broadcast_multiply_fusion.2), calls=%async_computation | async-start | bytes 131072 | tf_op jit(solution)/shard_map/all_to_all | solution.py:30
  72.7 3.9 %copy-start.1 = (f32[4096,128]{1,0:T(8,128)}, f32[4096,128]{1,0:T(8,128)S(1)}, u32[]{:S(2)}) copy-start(f32[4096,128]{1,0:T(8,128)S(1)} %scatter_fusion) | copy-start | bytes 6291460
where the time goes:
time: 77 us; the launch traced here: 76.6 us
  blocking collectives  37.7 us (49%)
  other arithmetic  20.3 us (26%)
  starting transfers between devices  7.29 us (9%)
  local copies, waits for them, and re-layouts  5.95 us (8%)
  waiting for transfers between devices  4.58 us (6%)
  between operations  0.79 us (1%)
    all_gather x1, blocking collectives, local(): lax.all_gather(out_values, 'dp', axis=0, tiled=True)  37.7 us
    all_to_all x1, starting transfers between devices, local(): lax.all_to_all(outgoing, 'dp', split_axis=0, concat_axis=0, tiled=True)  7.29 us
    all_to_all x1, waiting for transfers between devices, local(): lax.all_to_all(outgoing, 'dp', split_axis=0, concat_axis=0, tiled=True)  4.58 us
    sub x1, other arithmetic, local(): new_weights = weights - learning_rate * new_momentum  3.91 us
    mul x1, other arithmetic, local(): new_residual = (accumulated * (1.0 - my_mask * listed)[:, None])[None]  3.52 us
    scatter-add x1, other arithmetic, local(): blank.at[flat_lists]  2.68 us
    scatter-add x1, other arithmetic, local(): blank.at[owned_ids.reshape(-1)].add(incoming.reshape(-1, block_len))  2.41 us
    another operation x1, other arithmetic, local(): jnp.zeros((block_count,), jnp.float32).at[gath_idx.reshape(-1)]  2.29 us
  transfers between devices with their start and end apart: 1, of which 1 were waited for; matrix products, arithmetic and copies ran while one was open for 4% of the time, Pallas kernels for 0%

commit v1 on v0

v1 whole, which is shorter than its diff:
```python
import functools

import jax
import jax.numpy as jnp
from jax import lax
from jax.experimental import pallas as pl
from jax.experimental.pallas import tpu as pltpu
from jax.sharding import PartitionSpec as P

MESH = pl.DeviceIdType.MESH
momentum_coef = 0.9
learning_rate = 0.05
ROWS = 8


def exchange(
    n, chunk,
    grad, resid, weights, momentum, sel, counts, lists, list_counts,
    acc, mom, wts, kept, mrows, wrows, ids,
    res_buf, sel_s, cnt_s, gcnt_s, flags, outgoing, incoming, updates,
    load_sem, table_sem, send_sem, recv_sem, send2_sem, recv2_sem,
):
    me = lax.axis_index("dp")
    cap, list_len = sel_s.shape[0], ids.shape[0]
    block_count = acc.shape[0]

    band = pl.multiple_of((me // ROWS) * ROWS, ROWS)
    tables = [
        pltpu.make_async_copy(lists, ids, table_sem.at[0]),
        pltpu.make_async_copy(sel.at[me], sel_s, table_sem.at[1]),
        pltpu.make_async_copy(counts.at[pl.ds(band, ROWS)], cnt_s, table_sem.at[2]),
        pltpu.make_async_copy(list_counts, gcnt_s, table_sem.at[3]),
    ]
    loads = [
        pltpu.make_async_copy(grad, acc, load_sem.at[0]),
        pltpu.make_async_copy(resid, res_buf, load_sem.at[1]),
        pltpu.make_async_copy(momentum, mom, load_sem.at[2]),
        pltpu.make_async_copy(weights, wts, load_sem.at[3]),
    ]
    for copy in tables + loads:
        copy.start()

    barrier = pltpu.get_barrier_semaphore()

    def greet(k, _):
        pl.semaphore_signal(barrier, inc=1, device_id=(lax.rem(me + k, n),), device_id_type=MESH)
        return 0

    lax.fori_loop(1, n, greet, 0)

    for copy in tables:
        copy.wait()
    my_row = me - band

    def flag_owner(o, _):
        used = cnt_s[my_row, o]
        listed = gcnt_s[o]
        picks = [jnp.where(c < used, sel_s[c, o], -1) for c in range(cap)]
        for j in range(list_len):
            block = ids[j, o]
            hit = picks[0] == block
            for pick in picks[1:]:
                hit = jnp.logical_or(hit, pick == block)
            hit = jnp.logical_and(hit, j < listed)
            flags[j, o] = jnp.where(hit, jnp.float32(1.0), jnp.float32(0.0))
        return 0

    lax.fori_loop(0, n, flag_owner, 0)

    loads[0].wait()
    loads[1].wait()
    pl.semaphore_wait(barrier, n - 1)

    def pick_rows(o, target):
        for j in range(list_len):
            block = ids[j, o]
            row = acc[pl.ds(block, 1), :] + res_buf[pl.ds(block, 1), :]
            sent = row * flags[j, o]
            outgoing[o, pl.ds(j, 1), :] = sent
            if target is not None:
                target[o, pl.ds(j, 1), :] = sent
            kept[o, pl.ds(j, 1), :] = row - sent

    def send_to_owner(k, _):
        o = lax.rem(me + k, n)
        pick_rows(o, None)
        pltpu.make_async_remote_copy(
            src_ref=outgoing.at[o], dst_ref=incoming.at[me],
            send_sem=send_sem, recv_sem=recv_sem,
            device_id=(o,), device_id_type=MESH,
        ).start()
        return 0

    lax.fori_loop(1, n, send_to_owner, 0)
    pick_rows(me, incoming)

    def all_of(buffer, send, recv):
        part = buffer.at[pl.ds(0, n - 1)]
        return pltpu.make_async_remote_copy(
            src_ref=part, dst_ref=part, send_sem=send, recv_sem=recv,
            device_id=(lax.rem(me + 1, n),), device_id_type=MESH,
        )

    loads[2].wait()
    loads[3].wait()

    def pick_weights(o, _):
        for j in range(list_len):
            wrows[o, pl.ds(j, 1), :] = wts[pl.ds(ids[j, o], 1), :]
        return 0

    lax.fori_loop(0, n, pick_weights, 0)

    def dense_step(i, _):
        rows = pl.ds(pl.multiple_of(i * chunk, chunk), chunk)
        decayed = momentum_coef * mom[rows, :]
        mom[rows, :] = decayed
        wts[rows, :] = wts[rows, :] - learning_rate * decayed
        return 0

    lax.fori_loop(0, block_count // chunk, dense_step, 0)

    all_of(incoming, send_sem, recv_sem).wait_recv()
    updates[me] = jnp.sum(incoming[...], axis=0)

    def send_sum(k, _):
        pltpu.make_async_remote_copy(
            src_ref=updates.at[me], dst_ref=updates.at[me],
            send_sem=send2_sem, recv_sem=recv2_sem,
            device_id=(lax.rem(me + k, n),), device_id_type=MESH,
        ).start()
        return 0

    lax.fori_loop(1, n, send_sum, 0)

    def dense_acc(i, _):
        rows = pl.ds(pl.multiple_of(i * chunk, chunk), chunk)
        acc[rows, :] = acc[rows, :] + res_buf[rows, :]
        return 0

    lax.fori_loop(0, block_count // chunk, dense_acc, 0)

    def pick_momentum(o, _):
        for j in range(list_len):
            mrows[o, pl.ds(j, 1), :] = mom[pl.ds(ids[j, o], 1), :]
        return 0

    lax.fori_loop(0, n, pick_momentum, 0)

    all_of(outgoing, send_sem, recv_sem).wait_send()
    all_of(updates, send2_sem, recv2_sem).wait_recv()
    new_rows = mrows[...] + updates[...]
    mrows[...] = new_rows
    wrows[...] = wrows[...] - learning_rate * new_rows
    all_of(updates, send2_sem, recv2_sem).wait_send()


def finish(
    ids, acc_in, mom_in, wts_in, kept, mrows, wrows,
    new_weights, new_momentum, new_residual, acc, mom, wts,
    sems,
):
    n, list_len = kept.shape[0], kept.shape[1]
    copies = []
    for i, (rows, whole, result) in enumerate(
        ((kept, acc, new_residual), (mrows, mom, new_momentum), (wrows, wts, new_weights))
    ):
        def place(o, _, rows=rows, whole=whole):
            tile = rows[o]
            for j in range(list_len):
                whole[pl.ds(ids[j, o], 1), :] = tile[j:j + 1]
            return 0

        lax.fori_loop(0, n, place, 0)
        copies.append(pltpu.make_async_copy(whole, result, sems.at[i]))
        copies[-1].start()
    for copy in copies:
        copy.wait()


def local(n, gradient, residual, weights, momentum, sel_idx, sel_count, gath_idx, gath_count):
    block_count, block_len = weights.shape
    cap, list_len = sel_idx.shape[2], gath_idx.shape[1]
    f32, i32 = jnp.float32, jnp.int32
    dense = pltpu.VMEM((block_count, block_len), f32)
    tiles = pltpu.VMEM((n, list_len, block_len), f32)
    table = pltpu.SMEM((list_len, n), i32)
    any_space = pl.BlockSpec(memory_space=pl.ANY)
    vmem = pl.BlockSpec(memory_space=pltpu.VMEM)
    smem = pl.BlockSpec(memory_space=pltpu.SMEM)
    dense_bytes = block_count * block_len * 4
    tile_bytes = n * list_len * block_len * 4
    chunk = 64

    acc, mom, wts, kept, mrows, wrows, ids = pl.pallas_call(
        functools.partial(exchange, n, chunk),
        out_shape=(dense, dense, dense, tiles, tiles, tiles, table),
        in_specs=[any_space] * 8,
        out_specs=[vmem] * 6 + [smem],
        scratch_shapes=[
            dense,
            pltpu.SMEM((cap, n), i32),
            pltpu.SMEM((ROWS, n), i32),
            pltpu.SMEM((n,), i32),
            pltpu.SMEM((list_len, n), f32),
            tiles,
            tiles,
            tiles,
            pltpu.SemaphoreType.DMA((4,)),
            pltpu.SemaphoreType.DMA((4,)),
            pltpu.SemaphoreType.DMA,
            pltpu.SemaphoreType.DMA,
            pltpu.SemaphoreType.DMA,
            pltpu.SemaphoreType.DMA,
        ],
        compiler_params=pltpu.CompilerParams(
            collective_id=0, has_side_effects=True,
            vmem_limit_bytes=dense_bytes + 4 * tile_bytes + (1 << 21),
        ),
        cost_estimate=pl.CostEstimate(
            flops=5 * block_count * block_len, bytes_accessed=4 * dense_bytes, transcendentals=0
        ),
        name="exchange",
    )(
        gradient.reshape(block_count, block_len),
        residual.reshape(block_count, block_len),
        weights,
        momentum,
        sel_idx.transpose(0, 2, 1),
        sel_count,
        gath_idx.T,
        gath_count,
    )
    whole = jax.ShapeDtypeStruct((block_count, block_len), f32)
    new_weights, new_momentum, new_residual, _, _, _ = pl.pallas_call(
        finish,
        out_shape=(whole, whole, whole, dense, dense, dense),
        in_specs=[smem] + [vmem] * 6,
        out_specs=[any_space] * 3 + [vmem] * 3,
        input_output_aliases={1: 3, 2: 4, 3: 5},
        scratch_shapes=[pltpu.SemaphoreType.DMA((3,))],
        compiler_params=pltpu.CompilerParams(vmem_limit_bytes=1 << 21),
        cost_estimate=pl.CostEstimate(flops=0, bytes_accessed=3 * dense_bytes, transcendentals=0),
        name="finish",
    )(ids, acc, mom, wts, kept, mrows, wrows)
    return new_weights, new_momentum, new_residual[None]


def solution(mesh):
    placed = (P("dp", None, None), P("dp", None, None), P(), P(), P(), P(), P(), P())
    return jax.shard_map(
        functools.partial(local, mesh.shape["dp"]),
        mesh=mesh,
        in_specs=placed,
        out_specs=(P(), P(), P("dp", None, None)),
        check_vma=False,
    )
```

time: 77 us -> 31.7 us (0.41)
  blocking collectives: 37.7 us -> 0 us
  Pallas kernels: 0 us -> 21.4 us
  other arithmetic: 20.3 us -> 0 us
  starting transfers between devices: 7.29 us -> 0 us
  waiting for transfers between devices: 4.58 us -> 0 us
  local copies, waits for them, and re-layouts: 5.95 us -> 9.25 us
    all_gather x1 -> x0, blocking collectives: 37.7 us -> none  [local(): lax.all_gather(out_values, 'dp', axis=0, tiled=True)]
    pallas_call x0 -> x2, Pallas kernels: none -> 21.4 us  [the longest x1 18.2 us: local(): pl.pallas_call(functools.partial(exchange, n, chunk), out_shape=(dense, d...]
    unnamed x9 -> x16, local copies, waits for them, and re-layouts: 1.49 us -> 9.25 us
    all_to_all x1 -> x0, starting transfers between devices: 7.29 us -> none  [local(): lax.all_to_all(outgoing, 'dp', split_axis=0, concat_axis=0, tiled=True)]
    mul x4 -> x0, other arithmetic: 6.1 us -> none  [the longest x1 3.52 us: local(): new_residual = (accumulated * (1.0 - my_mask * listed)[:, None])[None]]
    scatter-add x2 -> x0, other arithmetic: 5.09 us -> none  [the longest x1 2.68 us: local(): blank.at[flat_lists]]
    all_to_all x1 -> x0, waiting for transfers between devices: 4.58 us -> none  [local(): lax.all_to_all(outgoing, 'dp', split_axis=0, concat_axis=0, tiled=True)]
    sub x2 -> x0, other arithmetic: 3.91 us -> none  [the longest x1 3.91 us: local(): new_weights = weights - learning_rate * new_momentum]
  transfers between devices with their start and end apart: 1 -> 0, of which waited for: 1 -> 0; matrix products, arithmetic and copies ran while one was open for 4% -> 0% of each run, Pallas kernels for 0% -> 0%
where the time goes in v1:
time: 31.7 us; the launch traced here: 31.3 us
  Pallas kernels  21.4 us (68%)
  local copies, waits for them, and re-layouts  9.25 us (29%)
  between operations  0.66 us (2%)
    pallas_call x1, Pallas kernels, local(): pl.pallas_call(functools.partial(exchange, n, chunk), out_shape=(dense, d...  18.2 us
    unnamed x16, local copies, waits for them, and re-layouts  9.25 us
    pallas_call x1, Pallas kernels, local(): pl.pallas_call(finish, out_shape=(whole, whole, whole, dense, dense, dens...  3.18 us

profile of v1, /device:TPU:0, one launch (start us, length us, event | category | flops | bytes accessed | tf_op | source)
XLA Modules:
  0.0 31.3 jit_solution(16229566811340011120)
XLA Ops:
  0.6 0.0 copy-start
  0.6 1.6 %copy-done = f32[1,4096,128]{2,1,0:T(8,128)S(1)} copy-done((f32[1,4096,128]{2,1,0:T(8,128)S(1)}, f32[1,4096,128]{2,1,0:T(8,128)}, u32[]{:S(2)}) %copy-start) | copy-done | bytes 2097176
  2.2 0.0 copy-start.1
  2.2 1.6 %copy-done.1 = f32[1,4096,128]{2,1,0:T(8,128)S(1)} copy-done((f32[1,4096,128]{2,1,0:T(8,128)S(1)}, f32[1,4096,128]{2,1,0:T(8,128)}, u32[]{:S(2)}) %copy-start.1) | copy-done | bytes 2097176
  3.8 0.0 copy-start.2
  3.8 1.6 %copy-done.2 = f32[4096,128]{1,0:T(8,128)S(1)} copy-done((f32[4096,128]{1,0:T(8,128)S(1)}, f32[4096,128]{1,0:T(8,128)}, u32[]{:S(2)}) %copy-start.2) | copy-done | bytes 2097176
  5.4 0.0 copy-start.3
  5.4 1.6 %copy-done.3 = f32[4096,128]{1,0:T(8,128)S(1)} copy-done((f32[4096,128]{1,0:T(8,128)S(1)}, f32[4096,128]{1,0:T(8,128)}, u32[]{:S(2)}) %copy-start.3) | copy-done | bytes 2097176
  7.0 0.0 copy-start.4
  7.0 0.8 %copy-done.4 = s32[32,32,4]{1,2,0:T(4,128)S(1)} copy-done((s32[32,32,4]{1,2,0:T(4,128)S(1)}, s32[32,32,4]{1,2,0:T(4,128)}, u32[]{:S(2)}) %copy-start.4) | copy-done | bytes 16408
  7.8 0.0 copy-start.5
  7.8 0.7 %copy-done.5 = s32[32,32]{1,0:T(8,128)S(1)} copy-done((s32[32,32]{1,0:T(8,128)S(1)}, s32[32,32]{1,0:T(8,128)}, u32[]{:S(2)}) %copy-start.5) | copy-done | bytes 4120
  8.6 0.0 copy-start.6
  8.6 0.7 %copy-done.6 = s32[32,8]{0,1:T(8,128)S(1)} copy-done((s32[32,8]{0,1:T(8,128)S(1)}, s32[32,8]{0,1:T(8,128)}, u32[]{:S(2)}) %copy-start.6) | copy-done | bytes 1048
  9.2 0.0 copy-start.7
  9.2 0.7 %copy-done.7 = s32[32]{0:T(128)S(1)} copy-done((s32[32]{0:T(128)S(1)}, s32[32]{0:T(128)}, u32[]{:S(2)}) %copy-start.7) | copy-done | bytes 152
  9.9 18.2 %exchange.1 = (f32[4096,128]{1,0:T(8,128)S(1)}, f32[4096,128]{1,0:T(8,128)S(1)}, f32[4096,128]{1,0:T(8,128)S(1)}, f32[32,8,128]{2,1,0:T(8,128)S(1)}, f32[32,8,12...) custom-call(f32[4096,128]{1,0:T(8,128)S(1)} %bitcast.5, f32[4096,128]{1,0:T(8,128)S(1)} %bitcast.6, ...), custom_call_target="tpu_custom_call" | custom-call | flops 2621440 | bytes 8388608 | tf_op jit(solution)/shard_map/exchange/pallas_call | solution.py:195
  28.1 3.2 %finish.1 = (f32[4096,128]{1,0:T(8,128)}, f32[4096,128]{1,0:T(8,128)}, f32[4096,128]{1,0:T(8,128)}, f32[4096,128]{1,0:T(8,128)S(1)}, f32[4096,128]{1,0:T(8,128)S(1)}, /*index=5*/f32[4096,128]{1,0:T(8,128)S(1)}) custom-call(s32[8,32]{1,0:T(8,128)S(4)} %get-tuple-element.13.ids, ...), custom_call_target="tpu_custom_call", output_to_operand_aliasing={{3}: (1, {}), {4}: (2, {}), {5}: (3, {})} | custom-call | bytes 6291456 | tf_op jit(solution)/shard_map/finish/pallas_call | solution.py:235
Async XLA Ops:
  0.6 1.6 %copy-start = (f32[1,4096,128]{2,1,0:T(8,128)S(1)}, f32[1,4096,128]{2,1,0:T(8,128)}, u32[]{:S(2)}) copy-start(f32[1,4096,128]{2,1,0:T(8,128)} %param.8) | copy-start | bytes 6291460
  2.2 1.6 %copy-start.1 = (f32[1,4096,128]{2,1,0:T(8,128)S(1)}, f32[1,4096,128]{2,1,0:T(8,128)}, u32[]{:S(2)}) copy-start(f32[1,4096,128]{2,1,0:T(8,128)} %param.9) | copy-start | bytes 6291460
  3.8 1.6 %copy-start.2 = (f32[4096,128]{1,0:T(8,128)S(1)}, f32[4096,128]{1,0:T(8,128)}, u32[]{:S(2)}) copy-start(f32[4096,128]{1,0:T(8,128)} %weights.1) | copy-start | bytes 6291460
  5.4 1.6 %copy-start.3 = (f32[4096,128]{1,0:T(8,128)S(1)}, f32[4096,128]{1,0:T(8,128)}, u32[]{:S(2)}) copy-start(f32[4096,128]{1,0:T(8,128)} %momentum.1) | copy-start | bytes 6291460
  7.0 0.8 %copy-start.4 = (s32[32,32,4]{1,2,0:T(4,128)S(1)}, s32[32,32,4]{1,2,0:T(4,128)}, u32[]{:S(2)}) copy-start(s32[32,32,4]{1,2,0:T(4,128)} %param.12) | copy-start | bytes 49156
  7.8 0.7 %copy-start.5 = (s32[32,32]{1,0:T(8,128)S(1)}, s32[32,32]{1,0:T(8,128)}, u32[]{:S(2)}) copy-start(s32[32,32]{1,0:T(8,128)} %counts.1) | copy-start | bytes 12292
  8.6 0.7 %copy-start.6 = (s32[32,8]{0,1:T(8,128)S(1)}, s32[32,8]{0,1:T(8,128)}, u32[]{:S(2)}) copy-start(s32[32,8]{0,1:T(8,128)} %param.14) | copy-start | bytes 3076
  9.2 0.7 %copy-start.7 = (s32[32]{0:T(128)S(1)}, s32[32]{0:T(128)}, u32[]{:S(2)}) copy-start(s32[32]{0:T(128)} %list_counts.1) | copy-start | bytes 388

commit v2 on v1

--- a/solution.py
+++ b/solution.py
@@ -11,6 +11,17 @@
 momentum_coef = 0.9
 learning_rate = 0.05
 ROWS = 8
+PIECES = 2
+
+
+def pieces(source, target, sems, first):
+    rows = source.shape[0] // PIECES
+    return [
+        pltpu.make_async_copy(
+            source.at[pl.ds(i * rows, rows)], target.at[pl.ds(i * rows, rows)], sems.at[first + i]
+        )
+        for i in range(PIECES)
+    ]
 
 
 def exchange(
@@ -31,19 +42,23 @@
         pltpu.make_async_copy(counts.at[pl.ds(band, ROWS)], cnt_s, table_sem.at[2]),
         pltpu.make_async_copy(list_counts, gcnt_s, table_sem.at[3]),
     ]
-    loads = [
-        pltpu.make_async_copy(grad, acc, load_sem.at[0]),
-        pltpu.make_async_copy(resid, res_buf, load_sem.at[1]),
-        pltpu.make_async_copy(momentum, mom, load_sem.at[2]),
-        pltpu.make_async_copy(weights, wts, load_sem.at[3]),
-    ]
-    for copy in tables + loads:
+
+    def load(source, target, first):
+        return pieces(source, target, load_sem, first)
+
+    first_loads = load(grad, acc, 0) + load(resid, res_buf, PIECES)
+    later_loads = load(momentum, mom, 2 * PIECES) + load(weights, wts, 3 * PIECES)
+    for copy in tables + first_loads:
         copy.start()
 
+    def peer(k):
+        raised = me + k
+        return jnp.where(raised >= n, raised - n, raised)
+
     barrier = pltpu.get_barrier_semaphore()
 
     def greet(k, _):
-        pl.semaphore_signal(barrier, inc=1, device_id=(lax.rem(me + k, n),), device_id_type=MESH)
+        pl.semaphore_signal(barrier, inc=1, device_id=(peer(k),), device_id_type=MESH)
         return 0
 
     lax.fori_loop(1, n, greet, 0)
@@ -67,8 +82,10 @@
 
     lax.fori_loop(0, n, flag_owner, 0)
 
-    loads[0].wait()
-    loads[1].wait()
+    for copy in first_loads:
+        copy.wait()
+    for copy in later_loads:
+        copy.start()
     pl.semaphore_wait(barrier, n - 1)
 
     def pick_rows(o, target):
@@ -82,7 +99,7 @@
             kept[o, pl.ds(j, 1), :] = row - sent
 
     def send_to_owner(k, _):
-        o = lax.rem(me + k, n)
+        o = peer(k)
         pick_rows(o, None)
         pltpu.make_async_remote_copy(
             src_ref=outgoing.at[o], dst_ref=incoming.at[me],
@@ -98,11 +115,11 @@
         part = buffer.at[pl.ds(0, n - 1)]
         return pltpu.make_async_remote_copy(
             src_ref=part, dst_ref=part, send_sem=send, recv_sem=recv,
-            device_id=(lax.rem(me + 1, n),), device_id_type=MESH,
+            device_id=(peer(1),), device_id_type=MESH,
         )
 
-    loads[2].wait()
-    loads[3].wait()
+    for copy in later_loads:
+        copy.wait()
 
     def pick_weights(o, _):
         for j in range(list_len):
@@ -127,7 +144,7 @@
         pltpu.make_async_remote_copy(
             src_ref=updates.at[me], dst_ref=updates.at[me],
             send_sem=send2_sem, recv_sem=recv2_sem,
-            device_id=(lax.rem(me + k, n),), device_id_type=MESH,
+            device_id=(peer(k),), device_id_type=MESH,
         ).start()
         return 0
 
@@ -162,18 +179,27 @@
 ):
     n, list_len = kept.shape[0], kept.shape[1]
     copies = []
-    for i, (rows, whole, result) in enumerate(
-        ((kept, acc, new_residual), (mrows, mom, new_momentum), (wrows, wts, new_weights))
-    ):
-        def place(o, _, rows=rows, whole=whole):
-            tile = rows[o]
+
+    def place(*pairs):
+        def step(o, _):
             for j in range(list_len):
-                whole[pl.ds(ids[j, o], 1), :] = tile[j:j + 1]
+                target = pl.ds(ids[j, o], 1)
+                for rows, whole in pairs:
+                    whole[target, :] = rows[o, pl.ds(j, 1), :]
             return 0
 
-        lax.fori_loop(0, n, place, 0)
-        copies.append(pltpu.make_async_copy(whole, result, sems.at[i]))
-        copies[-1].start()
+        lax.fori_loop(0, n, step, 0)
+
+    def write(whole, result):
+        copies.extend(pieces(whole, result, sems, len(copies)))
+        for copy in copies[-PIECES:]:
+            copy.start()
+
+    place((kept, acc))
+    write(acc, new_residual)
+    place((mrows, mom), (wrows, wts))
+    write(mom, new_momentum)
+    write(wts, new_weights)
     for copy in copies:
         copy.wait()
 
@@ -185,7 +211,7 @@
     dense = pltpu.VMEM((block_count, block_len), f32)
     tiles = pltpu.VMEM((n, list_len, block_len), f32)
     table = pltpu.SMEM((list_len, n), i32)
-    any_space = pl.BlockSpec(memory_space=pl.ANY)
+    hbm = pl.BlockSpec(memory_space=pltpu.HBM)
     vmem = pl.BlockSpec(memory_space=pltpu.VMEM)
     smem = pl.BlockSpec(memory_space=pltpu.SMEM)
     dense_bytes = block_count * block_len * 4
@@ -195,7 +221,7 @@
     acc, mom, wts, kept, mrows, wrows, ids = pl.pallas_call(
         functools.partial(exchange, n, chunk),
         out_shape=(dense, dense, dense, tiles, tiles, tiles, table),
-        in_specs=[any_space] * 8,
+        in_specs=[hbm] * 8,
         out_specs=[vmem] * 6 + [smem],
         scratch_shapes=[
             dense,
@@ -206,7 +232,7 @@
             tiles,
             tiles,
             tiles,
-            pltpu.SemaphoreType.DMA((4,)),
+            pltpu.SemaphoreType.DMA((4 * PIECES,)),
             pltpu.SemaphoreType.DMA((4,)),
             pltpu.SemaphoreType.DMA,
             pltpu.SemaphoreType.DMA,
@@ -221,24 +247,27 @@
             flops=5 * block_count * block_len, bytes_accessed=4 * dense_bytes, transcendentals=0
         ),
         name="exchange",
-    )(
-        gradient.reshape(block_count, block_len),
-        residual.reshape(block_count, block_len),
-        weights,
-        momentum,
-        sel_idx.transpose(0, 2, 1),
-        sel_count,
-        gath_idx.T,
-        gath_count,
-    )
+    )(*[
+        pltpu.with_memory_space_constraint(operand, pltpu.HBM)
+        for operand in (
+            gradient.reshape(block_count, block_len),
+            residual.reshape(block_count, block_len),
+            weights,
+            momentum,
+            sel_idx.transpose(0, 2, 1),
+            sel_count,
+            gath_idx.T,
+            gath_count,
+        )
+    ])
     whole = jax.ShapeDtypeStruct((block_count, block_len), f32)
     new_weights, new_momentum, new_residual, _, _, _ = pl.pallas_call(
         finish,
         out_shape=(whole, whole, whole, dense, dense, dense),
         in_specs=[smem] + [vmem] * 6,
-        out_specs=[any_space] * 3 + [vmem] * 3,
+        out_specs=[hbm] * 3 + [vmem] * 3,
         input_output_aliases={1: 3, 2: 4, 3: 5},
-        scratch_shapes=[pltpu.SemaphoreType.DMA((3,))],
+        scratch_shapes=[pltpu.SemaphoreType.DMA((3 * PIECES,))],
         compiler_params=pltpu.CompilerParams(vmem_limit_bytes=1 << 21),
         cost_estimate=pl.CostEstimate(flops=0, bytes_accessed=3 * dense_bytes, transcendentals=0),
         name="finish",

time: 31.7 us -> 21.7 us (0.68)
  local copies, waits for them, and re-layouts: 9.25 us -> 0 us
  Pallas kernels: 21.4 us -> 20.9 us
    unnamed x16 -> x0, local copies, waits for them, and re-layouts: 9.25 us -> none
    pallas_call x1, Pallas kernels: 18.2 us -> 17.7 us  [local(): pl.pallas_call(functools.partial(exchange, n, chunk), out_shape=(dense, d...]
where the time goes in v2:
time: 21.7 us; the launch traced here: 21.5 us
  Pallas kernels  20.9 us (96%)
  between operations  0.64 us (3%)
    pallas_call x1, Pallas kernels, local(): pl.pallas_call(functools.partial(exchange, n, chunk), out_shape=(dense, d...  17.7 us
    pallas_call x1, Pallas kernels, local(): pl.pallas_call(finish, out_shape=(whole, whole, whole, dense, dense, dens...  3.18 us

profile of v2, /device:TPU:0, one launch (start us, length us, event | category | flops | bytes accessed | tf_op | source)
XLA Modules:
  0.0 21.5 jit_solution(16478303165524278036)
XLA Ops:
  0.6 17.7 %exchange.1 = (f32[4096,128]{1,0:T(8,128)S(1)}, f32[4096,128]{1,0:T(8,128)S(1)}, f32[4096,128]{1,0:T(8,128)S(1)}, f32[32,8,128]{2,1,0:T(8,128)S(1)}, f32[32,8,12...) custom-call(f32[4096,128]{1,0:T(8,128)} %bitcast.5, f32[4096,128]{1,0:T(8,128)} %bitcast.6, ...), custom_call_target="tpu_custom_call" | custom-call | flops 2621440 | bytes 8388608 | tf_op jit(solution)/shard_map/exchange/pallas_call | solution.py:221
  18.3 3.2 %finish.1 = (f32[4096,128]{1,0:T(8,128)}, f32[4096,128]{1,0:T(8,128)}, f32[4096,128]{1,0:T(8,128)}, f32[4096,128]{1,0:T(8,128)S(1)}, f32[4096,128]{1,0:T(8,128)S(1)}, /*index=5*/f32[4096,128]{1,0:T(8,128)S(1)}) custom-call(s32[8,32]{1,0:T(8,128)S(4)} %get-tuple-element.13.ids, ...), custom_call_target="tpu_custom_call", output_to_operand_aliasing={{3}: (1, {}), {4}: (2, {}), {5}: (3, {})} | custom-call | bytes 6291456 | tf_op jit(solution)/shard_map/finish/pallas_call | solution.py:264

commit v3 on v2

--- a/solution.py
+++ b/solution.py
@@ -28,12 +28,21 @@
     n, chunk,
     grad, resid, weights, momentum, sel, counts, lists, list_counts,
     acc, mom, wts, kept, mrows, wrows, ids,
-    res_buf, sel_s, cnt_s, gcnt_s, flags, outgoing, incoming, updates,
-    load_sem, table_sem, send_sem, recv_sem, send2_sem, recv2_sem,
+    res_buf, sel_s, cnt_s, gcnt_s, flags, outgoing, beside, incoming, updates,
+    load_sem, table_sem, send_sems, recv_sems,
 ):
+    half = n // 2
     me = lax.axis_index("dp")
+    chip, core = me // 2, me % 2
+    other = 1 - core
+    sibling = 2 * chip + other
     cap, list_len = sel_s.shape[0], ids.shape[0]
     block_count = acc.shape[0]
+    mine, theirs = core * half, other * half
+
+    def chip_at(k):
+        raised = chip + k
+        return jnp.where(raised >= half, raised - half, raised)
 
     band = pl.multiple_of((me // ROWS) * ROWS, ROWS)
     tables = [
@@ -51,17 +60,16 @@
     for copy in tables + first_loads:
         copy.start()
 
-    def peer(k):
-        raised = me + k
-        return jnp.where(raised >= n, raised - n, raised)
-
     barrier = pltpu.get_barrier_semaphore()
 
     def greet(k, _):
-        pl.semaphore_signal(barrier, inc=1, device_id=(peer(k),), device_id_type=MESH)
-        return 0
-
-    lax.fori_loop(1, n, greet, 0)
+        pl.semaphore_signal(
+            barrier, inc=1, device_id=(2 * chip_at(k) + core,), device_id_type=MESH
+        )
+        return 0
+
+    lax.fori_loop(1, half, greet, 0)
+    pl.semaphore_signal(barrier, inc=1, device_id=(sibling,), device_id_type=MESH)
 
     for copy in tables:
         copy.wait()
@@ -86,47 +94,75 @@
         copy.wait()
     for copy in later_loads:
         copy.start()
-    pl.semaphore_wait(barrier, n - 1)
-
-    def pick_rows(o, target):
-        for j in range(list_len):
-            block = ids[j, o]
-            row = acc[pl.ds(block, 1), :] + res_buf[pl.ds(block, 1), :]
-            sent = row * flags[j, o]
-            outgoing[o, pl.ds(j, 1), :] = sent
-            if target is not None:
-                target[o, pl.ds(j, 1), :] = sent
-            kept[o, pl.ds(j, 1), :] = row - sent
+
+    def pick_for(side):
+        def pick_rows(c, _):
+            o, slot = 2 * c + side, side * half + c
+            for j in range(list_len):
+                block = ids[j, o]
+                row = acc[pl.ds(block, 1), :] + res_buf[pl.ds(block, 1), :]
+                sent = row * flags[j, o]
+                outgoing[slot, pl.ds(j, 1), :] = sent
+                kept[slot, pl.ds(j, 1), :] = row - sent
+            return 0
+
+        lax.fori_loop(0, half, pick_rows, 0)
+
+    def remote(source, target, phase, device):
+        return pltpu.make_async_remote_copy(
+            src_ref=source, dst_ref=target,
+            send_sem=send_sems.at[phase], recv_sem=recv_sems.at[phase],
+            device_id=(device,), device_id_type=MESH,
+        )
+
+    pick_for(other)
+    pl.semaphore_wait(barrier, half)
+    swap = remote(outgoing.at[pl.ds(theirs, half)], beside, 0, sibling)
+    swap.start()
+    pick_for(core)
+    swap.wait_recv()
 
     def send_to_owner(k, _):
-        o = peer(k)
-        pick_rows(o, None)
-        pltpu.make_async_remote_copy(
-            src_ref=outgoing.at[o], dst_ref=incoming.at[me],
-            send_sem=send_sem, recv_sem=recv_sem,
-            device_id=(o,), device_id_type=MESH,
-        ).start()
-        return 0
-
-    lax.fori_loop(1, n, send_to_owner, 0)
-    pick_rows(me, incoming)
-
-    def all_of(buffer, send, recv):
-        part = buffer.at[pl.ds(0, n - 1)]
-        return pltpu.make_async_remote_copy(
-            src_ref=part, dst_ref=part, send_sem=send, recv_sem=recv,
-            device_id=(peer(1),), device_id_type=MESH,
-        )
+        c = chip_at(k)
+        outgoing[mine + c] = outgoing[mine + c] + beside[c]
+        remote(outgoing.at[mine + c], incoming.at[chip], 1, 2 * c + core).start()
+        return 0
+
+    lax.fori_loop(1, half, send_to_owner, 0)
+    incoming[chip] = outgoing[mine + chip] + beside[chip]
+
+    def all_peers(phase):
+        part = incoming.at[pl.ds(0, half - 1)]
+        return remote(part, part, phase, sibling)
+
+    def dense_acc(i, _):
+        rows = pl.ds(pl.multiple_of(i * chunk, chunk), chunk)
+        acc[rows, :] = acc[rows, :] + res_buf[rows, :]
+        return 0
+
+    lax.fori_loop(0, block_count // chunk, dense_acc, 0)
+    all_peers(1).wait_recv()
+    updates[mine + chip] = jnp.sum(incoming[...], axis=0)
+
+    def send_sum(k, _):
+        own = updates.at[mine + chip]
+        remote(own, own, 2, 2 * chip_at(k) + core).start()
+        return 0
+
+    lax.fori_loop(1, half, send_sum, 0)
 
     for copy in later_loads:
         copy.wait()
 
-    def pick_weights(o, _):
-        for j in range(list_len):
-            wrows[o, pl.ds(j, 1), :] = wts[pl.ds(ids[j, o], 1), :]
-        return 0
-
-    lax.fori_loop(0, n, pick_weights, 0)
+    def pick_weights(c, _):
+        for side in range(2):
+            for j in range(list_len):
+                block = pl.ds(ids[j, 2 * c + side], 1)
+                wrows[side * half + c, pl.ds(j, 1), :] = wts[block, :]
+                mrows[side * half + c, pl.ds(j, 1), :] = mom[block, :]
+        return 0
+
+    lax.fori_loop(0, half, pick_weights, 0)
 
     def dense_step(i, _):
         rows = pl.ds(pl.multiple_of(i * chunk, chunk), chunk)
@@ -137,39 +173,23 @@
 
     lax.fori_loop(0, block_count // chunk, dense_step, 0)
 
-    all_of(incoming, send_sem, recv_sem).wait_recv()
-    updates[me] = jnp.sum(incoming[...], axis=0)
-
-    def send_sum(k, _):
-        pltpu.make_async_remote_copy(
-            src_ref=updates.at[me], dst_ref=updates.at[me],
-            send_sem=send2_sem, recv_sem=recv2_sem,
-            device_id=(peer(k),), device_id_type=MESH,
-        ).start()
-        return 0
-
-    lax.fori_loop(1, n, send_sum, 0)
-
-    def dense_acc(i, _):
-        rows = pl.ds(pl.multiple_of(i * chunk, chunk), chunk)
-        acc[rows, :] = acc[rows, :] + res_buf[rows, :]
-        return 0
-
-    lax.fori_loop(0, block_count // chunk, dense_acc, 0)
-
-    def pick_momentum(o, _):
-        for j in range(list_len):
-            mrows[o, pl.ds(j, 1), :] = mom[pl.ds(ids[j, o], 1), :]
-        return 0
-
-    lax.fori_loop(0, n, pick_momentum, 0)
-
-    all_of(outgoing, send_sem, recv_sem).wait_send()
-    all_of(updates, send2_sem, recv2_sem).wait_recv()
-    new_rows = mrows[...] + updates[...]
-    mrows[...] = new_rows
-    wrows[...] = wrows[...] - learning_rate * new_rows
-    all_of(updates, send2_sem, recv2_sem).wait_send()
+    def apply_sums(first):
+        part = pl.ds(first, half)
+        new_rows = momentum_coef * mrows[part] + updates[part]
+        mrows[part] = new_rows
+        wrows[part] = wrows[part] - learning_rate * new_rows
+
+    all_peers(2).wait_recv()
+    own_side = updates.at[pl.ds(mine, half)]
+    relay = remote(own_side, own_side, 3, sibling)
+    relay.start()
+    apply_sums(mine)
+    swap.wait_send()
+    all_peers(1).wait_send()
+    all_peers(2).wait_send()
+    relay.wait_recv()
+    apply_sums(theirs)
+    relay.wait_send()
 
 
 def finish(
@@ -177,18 +197,19 @@
     new_weights, new_momentum, new_residual, acc, mom, wts,
     sems,
 ):
-    n, list_len = kept.shape[0], kept.shape[1]
+    half, list_len = kept.shape[0] // 2, kept.shape[1]
     copies = []
 
     def place(*pairs):
-        def step(o, _):
-            for j in range(list_len):
-                target = pl.ds(ids[j, o], 1)
-                for rows, whole in pairs:
-                    whole[target, :] = rows[o, pl.ds(j, 1), :]
+        def step(c, _):
+            for side in range(2):
+                for j in range(list_len):
+                    target = pl.ds(ids[j, 2 * c + side], 1)
+                    for rows, whole in pairs:
+                        whole[target, :] = rows[side * half + c, pl.ds(j, 1), :]
             return 0
 
-        lax.fori_loop(0, n, step, 0)
+        lax.fori_loop(0, half, step, 0)
 
     def write(whole, result):
         copies.extend(pieces(whole, result, sems, len(copies)))
@@ -210,6 +231,7 @@
     f32, i32 = jnp.float32, jnp.int32
     dense = pltpu.VMEM((block_count, block_len), f32)
     tiles = pltpu.VMEM((n, list_len, block_len), f32)
+    half_tiles = pltpu.VMEM((n // 2, list_len, block_len), f32)
     table = pltpu.SMEM((list_len, n), i32)
     hbm = pl.BlockSpec(memory_space=pltpu.HBM)
     vmem = pl.BlockSpec(memory_space=pltpu.VMEM)
@@ -230,14 +252,13 @@
             pltpu.SMEM((n,), i32),
             pltpu.SMEM((list_len, n), f32),
             tiles,
-            tiles,
+            half_tiles,
+            half_tiles,
             tiles,
             pltpu.SemaphoreType.DMA((4 * PIECES,)),
             pltpu.SemaphoreType.DMA((4,)),
-            pltpu.SemaphoreType.DMA,
-            pltpu.SemaphoreType.DMA,
-            pltpu.SemaphoreType.DMA,
-            pltpu.SemaphoreType.DMA,
+            pltpu.SemaphoreType.DMA((4,)),
+            pltpu.SemaphoreType.DMA((4,)),
         ],
         compiler_params=pltpu.CompilerParams(
             collective_id=0, has_side_effects=True,

time: 21.7 us -> 22.1 us (1.018)
  Pallas kernels: 20.9 us -> 21.3 us
    pallas_call x1, Pallas kernels: 17.7 us -> 18.1 us  [local(): pl.pallas_call(functools.partial(exchange, n, chunk), out_shape=(dense, d...]
where the time goes in v3:
time: 22.1 us; the launch traced here: 21.9 us
  Pallas kernels  21.3 us (96%)
  between operations  0.64 us (3%)
    pallas_call x1, Pallas kernels, local(): pl.pallas_call(functools.partial(exchange, n, chunk), out_shape=(dense, d...  18.1 us
    pallas_call x1, Pallas kernels, local(): pl.pallas_call(finish, out_shape=(whole, whole, whole, dense, dense, dens...  3.15 us

profile of v3, /device:TPU:0, one launch (start us, length us, event | category | flops | bytes accessed | tf_op | source)
XLA Modules:
  0.0 21.9 jit_solution(8269680693213607137)
XLA Ops:
  0.6 18.1 %exchange.1 = (f32[4096,128]{1,0:T(8,128)S(1)}, f32[4096,128]{1,0:T(8,128)S(1)}, f32[4096,128]{1,0:T(8,128)S(1)}, f32[32,8,128]{2,1,0:T(8,128)S(1)}, f32[32,8,12...) custom-call(f32[4096,128]{1,0:T(8,128)} %bitcast.5, f32[4096,128]{1,0:T(8,128)} %bitcast.6, ...), custom_call_target="tpu_custom_call" | custom-call | flops 2621440 | bytes 8388608 | tf_op jit(solution)/shard_map/exchange/pallas_call | solution.py:243
  18.8 3.2 %finish.1 = (f32[4096,128]{1,0:T(8,128)}, f32[4096,128]{1,0:T(8,128)}, f32[4096,128]{1,0:T(8,128)}, f32[4096,128]{1,0:T(8,128)S(1)}, f32[4096,128]{1,0:T(8,128)S(1)}, /*index=5*/f32[4096,128]{1,0:T(8,128)S(1)}) custom-call(s32[8,32]{1,0:T(8,128)S(4)} %get-tuple-element.13.ids, ...), custom_call_target="tpu_custom_call", output_to_operand_aliasing={{3}: (1, {}), {4}: (2, {}), {5}: (3, {})} | custom-call | bytes 6291456 | tf_op jit(solution)/shard_map/finish/pallas_call | solution.py:285

commit v4 on v3

--- a/solution.py
+++ b/solution.py
@@ -28,7 +28,7 @@
     n, chunk,
     grad, resid, weights, momentum, sel, counts, lists, list_counts,
     acc, mom, wts, kept, mrows, wrows, ids,
-    res_buf, sel_s, cnt_s, gcnt_s, flags, outgoing, beside, incoming, updates,
+    res_buf, sel_v, cnt_v, gcnt_v, ids_v, flags_v, flags, outgoing, beside, incoming, updates,
     load_sem, table_sem, send_sems, recv_sems,
 ):
     half = n // 2
@@ -36,7 +36,7 @@
     chip, core = me // 2, me % 2
     other = 1 - core
     sibling = 2 * chip + other
-    cap, list_len = sel_s.shape[0], ids.shape[0]
+    cap, list_len = sel_v.shape[0], ids.shape[0]
     block_count = acc.shape[0]
     mine, theirs = core * half, other * half
 
@@ -47,9 +47,10 @@
     band = pl.multiple_of((me // ROWS) * ROWS, ROWS)
     tables = [
         pltpu.make_async_copy(lists, ids, table_sem.at[0]),
-        pltpu.make_async_copy(sel.at[me], sel_s, table_sem.at[1]),
-        pltpu.make_async_copy(counts.at[pl.ds(band, ROWS)], cnt_s, table_sem.at[2]),
-        pltpu.make_async_copy(list_counts, gcnt_s, table_sem.at[3]),
+        pltpu.make_async_copy(sel.at[me], sel_v, table_sem.at[1]),
+        pltpu.make_async_copy(counts.at[pl.ds(band, ROWS)], cnt_v, table_sem.at[2]),
+        pltpu.make_async_copy(list_counts, gcnt_v, table_sem.at[3]),
+        pltpu.make_async_copy(lists, ids_v, table_sem.at[4]),
     ]
 
     def load(source, target, first):
@@ -73,37 +74,33 @@
 
     for copy in tables:
         copy.wait()
-    my_row = me - band
-
-    def flag_owner(o, _):
-        used = cnt_s[my_row, o]
-        listed = gcnt_s[o]
-        picks = [jnp.where(c < used, sel_s[c, o], -1) for c in range(cap)]
-        for j in range(list_len):
-            block = ids[j, o]
-            hit = picks[0] == block
-            for pick in picks[1:]:
-                hit = jnp.logical_or(hit, pick == block)
-            hit = jnp.logical_and(hit, j < listed)
-            flags[j, o] = jnp.where(hit, jnp.float32(1.0), jnp.float32(0.0))
-        return 0
-
-    lax.fori_loop(0, n, flag_owner, 0)
+    used = cnt_v[pl.ds(me - band, 1), :]
+    listed = gcnt_v[...].reshape(1, n)
+    blocks = ids_v[...]
+    hit = jnp.zeros((list_len, n), jnp.float32)
+    for c in range(cap):
+        picked = jnp.where(c < used, sel_v[pl.ds(c, 1), :], -1)
+        hit = jnp.where(blocks == picked, 1.0, hit)
+    slots = lax.broadcasted_iota(jnp.int32, (list_len, n), 0)
+    flags_v[...] = jnp.where(slots < listed, hit, 0.0)
+    flag_copy = pltpu.make_async_copy(flags_v, flags, table_sem.at[0])
+    flag_copy.start()
 
     for copy in first_loads:
         copy.wait()
     for copy in later_loads:
         copy.start()
+    flag_copy.wait()
 
     def pick_for(side):
         def pick_rows(c, _):
             o, slot = 2 * c + side, side * half + c
+            rows = [pl.ds(ids[j, o], 1) for j in range(list_len)]
+            rows = [acc[row, :] + res_buf[row, :] for row in rows]
+            sent = [row * flags[j, o] for j, row in enumerate(rows)]
             for j in range(list_len):
-                block = ids[j, o]
-                row = acc[pl.ds(block, 1), :] + res_buf[pl.ds(block, 1), :]
-                sent = row * flags[j, o]
-                outgoing[slot, pl.ds(j, 1), :] = sent
-                kept[slot, pl.ds(j, 1), :] = row - sent
+                outgoing[slot, pl.ds(j, 1), :] = sent[j]
+                kept[slot, pl.ds(j, 1), :] = rows[j] - sent[j]
             return 0
 
         lax.fori_loop(0, half, pick_rows, 0)
@@ -155,11 +152,12 @@
         copy.wait()
 
     def pick_weights(c, _):
-        for side in range(2):
-            for j in range(list_len):
-                block = pl.ds(ids[j, 2 * c + side], 1)
-                wrows[side * half + c, pl.ds(j, 1), :] = wts[block, :]
-                mrows[side * half + c, pl.ds(j, 1), :] = mom[block, :]
+        places = [(side, j) for side in range(2) for j in range(list_len)]
+        blocks = [pl.ds(ids[j, 2 * c + side], 1) for side, j in places]
+        found = [(wts[block, :], mom[block, :]) for block in blocks]
+        for (side, j), (weight, moment) in zip(places, found):
+            wrows[side * half + c, pl.ds(j, 1), :] = weight
+            mrows[side * half + c, pl.ds(j, 1), :] = moment
         return 0
 
     lax.fori_loop(0, half, pick_weights, 0)
@@ -202,11 +200,12 @@
 
     def place(*pairs):
         def step(c, _):
-            for side in range(2):
-                for j in range(list_len):
-                    target = pl.ds(ids[j, 2 * c + side], 1)
-                    for rows, whole in pairs:
-                        whole[target, :] = rows[side * half + c, pl.ds(j, 1), :]
+            places = [(side, j) for side in range(2) for j in range(list_len)]
+            targets = [pl.ds(ids[j, 2 * c + side], 1) for side, j in places]
+            for rows, whole in pairs:
+                values = [rows[side * half + c, pl.ds(j, 1), :] for side, j in places]
+                for target, value in zip(targets, values):
+                    whole[target, :] = value
             return 0
 
         lax.fori_loop(0, half, step, 0)
@@ -238,7 +237,7 @@
     smem = pl.BlockSpec(memory_space=pltpu.SMEM)
     dense_bytes = block_count * block_len * 4
     tile_bytes = n * list_len * block_len * 4
-    chunk = 64
+    chunk = 256
 
     acc, mom, wts, kept, mrows, wrows, ids = pl.pallas_call(
         functools.partial(exchange, n, chunk),
@@ -247,16 +246,18 @@
         out_specs=[vmem] * 6 + [smem],
         scratch_shapes=[
             dense,
-            pltpu.SMEM((cap, n), i32),
-            pltpu.SMEM((ROWS, n), i32),
-            pltpu.SMEM((n,), i32),
+            pltpu.VMEM((cap, n), i32),
+            pltpu.VMEM((ROWS, n), i32),
+            pltpu.VMEM((n,), i32),
+            pltpu.VMEM((list_len, n), i32),
+            pltpu.VMEM((list_len, n), f32),
             pltpu.SMEM((list_len, n), f32),
             tiles,
             half_tiles,
             half_tiles,
             tiles,
             pltpu.SemaphoreType.DMA((4 * PIECES,)),
-            pltpu.SemaphoreType.DMA((4,)),
+            pltpu.SemaphoreType.DMA((5,)),
             pltpu.SemaphoreType.DMA((4,)),
             pltpu.SemaphoreType.DMA((4,)),
         ],

time: 22.1 us -> 22 us (level)
  no operation moved by 1% of the time
where the time goes in v4:
time: 22 us; the launch traced here: 21.9 us
  Pallas kernels  21.2 us (96%)
  between operations  0.64 us (3%)
    pallas_call x1, Pallas kernels, local(): pl.pallas_call(functools.partial(exchange, n, chunk), out_shape=(dense, d...  18.1 us
    pallas_call x1, Pallas kernels, local(): pl.pallas_call(finish, out_shape=(whole, whole, whole, dense, dense, dens...  3.15 us

profile of v4, /device:TPU:0, one launch (start us, length us, event | category | flops | bytes accessed | tf_op | source)
XLA Modules:
  0.0 21.9 jit_solution(11425744538173591881)
XLA Ops:
  0.6 18.1 %exchange.1 = (f32[4096,128]{1,0:T(8,128)S(1)}, f32[4096,128]{1,0:T(8,128)S(1)}, f32[4096,128]{1,0:T(8,128)S(1)}, f32[32,8,128]{2,1,0:T(8,128)S(1)}, f32[32,8,12...) custom-call(f32[4096,128]{1,0:T(8,128)} %bitcast.5, f32[4096,128]{1,0:T(8,128)} %bitcast.6, ...), custom_call_target="tpu_custom_call" | custom-call | flops 2621440 | bytes 8388608 | tf_op jit(solution)/shard_map/exchange/pallas_call | solution.py:242
  18.7 3.2 %finish.1 = (f32[4096,128]{1,0:T(8,128)}, f32[4096,128]{1,0:T(8,128)}, f32[4096,128]{1,0:T(8,128)}, f32[4096,128]{1,0:T(8,128)S(1)}, f32[4096,128]{1,0:T(8,128)S(1)}, /*index=5*/f32[4096,128]{1,0:T(8,128)S(1)}) custom-call(s32[8,32]{1,0:T(8,128)S(4)} %get-tuple-element.13.ids, ...), custom_call_target="tpu_custom_call", output_to_operand_aliasing={{3}: (1, {}), {4}: (2, {}), {5}: (3, {})} | custom-call | bytes 6291456 | tf_op jit(solution)/shard_map/finish/pallas_call | solution.py:286

commit v5 on v4

v5 whole, which is shorter than its diff:
```python
import functools

import jax
import jax.numpy as jnp
from jax import lax
from jax.experimental import pallas as pl
from jax.experimental.pallas import tpu as pltpu
from jax.sharding import PartitionSpec as P

MESH = pl.DeviceIdType.MESH
momentum_coef = 0.9
learning_rate = 0.05
ROWS = 8
PIECES = 2


def pieces(source, target, sems, first):
    rows = source.shape[0] // PIECES
    return [
        pltpu.make_async_copy(
            source.at[pl.ds(i * rows, rows)], target.at[pl.ds(i * rows, rows)], sems.at[first + i]
        )
        for i in range(PIECES)
    ]


def exchange(
    n, chunk,
    grad, resid, weights, momentum, sel, counts, lists, list_counts,
    acc, mom, wts, kept, mrows, wrows, ids,
    res_buf, sel_s, cnt_s, gcnt_s, flags, sel_v, cnt_v, gcnt_v, ids_v, flags_v,
    outgoing, incoming, sender_blocks, updates,
    load_sem, table_sem, send_sems, recv_sems,
):
    me = lax.axis_index("dp")
    cap, list_len = sel_s.shape[0], ids.shape[0]
    block_count, block_len = acc.shape

    band = pl.multiple_of((me // ROWS) * ROWS, ROWS)
    tables = [
        pltpu.make_async_copy(source, target, table_sem.at[i])
        for i, (source, target) in enumerate((
            (lists, ids), (sel.at[me], sel_s), (counts.at[pl.ds(band, ROWS)], cnt_s), (list_counts, gcnt_s),
            (sel, sel_v), (counts.at[pl.ds(band, ROWS)], cnt_v), (list_counts, gcnt_v), (lists, ids_v),
        ))
    ]

    def load(source, target, first):
        return pieces(source, target, load_sem, first)

    first_loads = load(grad, acc, 0) + load(resid, res_buf, PIECES)
    later_loads = load(momentum, mom, 2 * PIECES) + load(weights, wts, 3 * PIECES)
    for copy in tables[:4] + first_loads + tables[4:]:
        copy.start()

    bits = [1 << i for i in range((n - 1).bit_length())]
    my_bits = [(me // bit) % 2 for bit in bits]

    def peer(step):
        k = n - step
        both = sum(mine * ((k // bit) % 2) * bit for mine, bit in zip(my_bits, bits))
        return me + k - 2 * both

    barrier = pltpu.get_barrier_semaphore()

    def greet(step, _):
        pl.semaphore_signal(barrier, inc=1, device_id=(peer(step),), device_id_type=MESH)
        return 0

    lax.fori_loop(1, n, greet, 0)

    for copy in tables:
        copy.wait()
    my_row = me - band
    used = cnt_v[pl.ds(my_row, 1), :]
    listed = gcnt_v[...].reshape(1, n)
    blocks = ids_v[...]
    selected = sel_v[me]
    hit = jnp.zeros((list_len, n), jnp.float32)
    for c in range(cap):
        picked = jnp.where(c < used, selected[c:c + 1, :], -1)
        hit = jnp.where(blocks == picked, 1.0, hit)
    slots = lax.broadcasted_iota(jnp.int32, (list_len, n), 0)
    flags_v[...] = jnp.where(slots < listed, hit, 0.0)
    flag_copy = pltpu.make_async_copy(flags_v, flags, table_sem.at[0])
    flag_copy.start()
    lanes = lax.broadcasted_iota(jnp.int32, (n, cap, n), 2)
    for_me = jnp.where(lanes == me, sel_v[...].astype(jnp.float32), 0.0)
    sender_blocks[...] = jnp.broadcast_to(
        jnp.sum(for_me, axis=2, keepdims=True), (n, cap, block_len)
    )

    for copy in first_loads:
        copy.wait()
    for copy in later_loads:
        copy.start()

    def pick_rows(o, _):
        rows = [pl.ds(sel_s[c, o], 1) for c in range(cap)]
        rows = [acc[row, :] + res_buf[row, :] for row in rows]
        count = cnt_s[my_row, o]
        for c in range(cap):
            outgoing[o, pl.ds(c, 1), :] = rows[c] * jnp.where(c < count, 1.0, 0.0)
        return 0

    lax.fori_loop(0, n, pick_rows, 0)

    def remote(source, target, phase, device):
        return pltpu.make_async_remote_copy(
            src_ref=source, dst_ref=target,
            send_sem=send_sems.at[phase], recv_sem=recv_sems.at[phase],
            device_id=(device,), device_id_type=MESH,
        )

    def all_peers(buffer, phase):
        part = buffer.at[pl.ds(0, n - 1)]
        return remote(part, part, phase, peer(1))

    pl.semaphore_wait(barrier, n - 1)

    def send_to_owner(step, _):
        o = peer(step)
        remote(outgoing.at[o], incoming.at[me], 0, o).start()
        return 0

    lax.fori_loop(1, n, send_to_owner, 0)
    incoming[me] = outgoing[me]

    def dense_acc(i, _):
        rows = pl.ds(pl.multiple_of(i * chunk, chunk), chunk)
        acc[rows, :] = acc[rows, :] + res_buf[rows, :]
        return 0

    lax.fori_loop(0, block_count // chunk, dense_acc, 0)
    my_count = gcnt_s[me]
    all_peers(incoming, 0).wait_recv()
    for j in range(list_len):
        block = jnp.where(j < my_count, ids[j, me], -1).astype(jnp.float32)
        chosen = jnp.where(sender_blocks[...] == block, incoming[...], 0.0)
        updates[me, pl.ds(j, 1), :] = jnp.sum(jnp.sum(chosen, axis=0), axis=0, keepdims=True)

    def send_sum(step, _):
        remote(updates.at[me], updates.at[me], 1, peer(step)).start()
        return 0

    lax.fori_loop(1, n, send_sum, 0)
    flag_copy.wait()

    def pick_kept(o, _):
        rows = [acc[pl.ds(ids[j, o], 1), :] for j in range(list_len)]
        for j in range(list_len):
            kept[o, pl.ds(j, 1), :] = rows[j] * (1.0 - flags[j, o])
        return 0

    lax.fori_loop(0, n, pick_kept, 0)
    for copy in later_loads:
        copy.wait()

    def pick_weights(o, _):
        blocks = [pl.ds(ids[j, o], 1) for j in range(list_len)]
        found = [(wts[block, :], mom[block, :]) for block in blocks]
        for j, (weight, moment) in enumerate(found):
            wrows[o, pl.ds(j, 1), :] = weight
            mrows[o, pl.ds(j, 1), :] = moment
        return 0

    lax.fori_loop(0, n, pick_weights, 0)

    def dense_step(i, _):
        rows = pl.ds(pl.multiple_of(i * chunk, chunk), chunk)
        decayed = momentum_coef * mom[rows, :]
        mom[rows, :] = decayed
        wts[rows, :] = wts[rows, :] - learning_rate * decayed
        return 0

    lax.fori_loop(0, block_count // chunk, dense_step, 0)
    all_peers(outgoing, 0).wait_send()
    all_peers(updates, 1).wait_recv()
    new_rows = momentum_coef * mrows[...] + updates[...]
    mrows[...] = new_rows
    wrows[...] = wrows[...] - learning_rate * new_rows
    all_peers(updates, 1).wait_send()


def finish(
    ids, acc_in, mom_in, wts_in, kept, mrows, wrows,
    new_weights, new_momentum, new_residual, acc, mom, wts,
    sems,
):
    half, list_len = kept.shape[0] // 2, kept.shape[1]
    copies = []

    def place(*pairs):
        def step(c, _):
            places = [(side, j) for side in range(2) for j in range(list_len)]
            targets = [pl.ds(ids[j, 2 * c + side], 1) for side, j in places]
            for rows, whole in pairs:
                values = [rows[2 * c + side, pl.ds(j, 1), :] for side, j in places]
                for target, value in zip(targets, values):
                    whole[target, :] = value
            return 0

        lax.fori_loop(0, half, step, 0)

    def write(whole, result):
        copies.extend(pieces(whole, result, sems, len(copies)))
        for copy in copies[-PIECES:]:
            copy.start()

    place((kept, acc))
    write(acc, new_residual)
    place((mrows, mom), (wrows, wts))
    write(mom, new_momentum)
    write(wts, new_weights)
    for copy in copies:
        copy.wait()


def local(n, gradient, residual, weights, momentum, sel_idx, sel_count, gath_idx, gath_count):
    block_count, block_len = weights.shape
    cap, list_len = sel_idx.shape[2], gath_idx.shape[1]
    f32, i32 = jnp.float32, jnp.int32
    dense = pltpu.VMEM((block_count, block_len), f32)
    tiles = pltpu.VMEM((n, list_len, block_len), f32)
    picks = pltpu.VMEM((n, cap, block_len), f32)
    table = pltpu.SMEM((list_len, n), i32)
    hbm = pl.BlockSpec(memory_space=pltpu.HBM)
    vmem = pl.BlockSpec(memory_space=pltpu.VMEM)
    smem = pl.BlockSpec(memory_space=pltpu.SMEM)
    dense_bytes = block_count * block_len * 4
    tile_bytes = n * list_len * block_len * 4
    chunk = 256

    acc, mom, wts, kept, mrows, wrows, ids = pl.pallas_call(
        functools.partial(exchange, n, chunk),
        out_shape=(dense, dense, dense, tiles, tiles, tiles, table),
        in_specs=[hbm] * 8,
        out_specs=[vmem] * 6 + [smem],
        scratch_shapes=[
            dense,
            pltpu.SMEM((cap, n), i32),
            pltpu.SMEM((ROWS, n), i32),
            pltpu.SMEM((n,), i32),
            pltpu.SMEM((list_len, n), f32),
            pltpu.VMEM((n, cap, n), i32),
            pltpu.VMEM((ROWS, n), i32),
            pltpu.VMEM((n,), i32),
            pltpu.VMEM((list_len, n), i32),
            pltpu.VMEM((list_len, n), f32),
            picks,
            picks,
            picks,
            tiles,
            pltpu.SemaphoreType.DMA((4 * PIECES,)),
            pltpu.SemaphoreType.DMA((8,)),
            pltpu.SemaphoreType.DMA((2,)),
            pltpu.SemaphoreType.DMA((2,)),
        ],
        compiler_params=pltpu.CompilerParams(
            collective_id=0, has_side_effects=True,
            vmem_limit_bytes=dense_bytes + 8 * tile_bytes + (1 << 21),
        ),
        cost_estimate=pl.CostEstimate(
            flops=5 * block_count * block_len, bytes_accessed=4 * dense_bytes, transcendentals=0
        ),
        name="exchange",
    )(*[
        pltpu.with_memory_space_constraint(operand, pltpu.HBM)
        for operand in (
            gradient.reshape(block_count, block_len),
            residual.reshape(block_count, block_len),
            weights,
            momentum,
            sel_idx.transpose(0, 2, 1),
            sel_count,
            gath_idx.T,
            gath_count,
        )
    ])
    whole = jax.ShapeDtypeStruct((block_count, block_len), f32)
    new_weights, new_momentum, new_residual, _, _, _ = pl.pallas_call(
        finish,
        out_shape=(whole, whole, whole, dense, dense, dense),
        in_specs=[smem] + [vmem] * 6,
        out_specs=[hbm] * 3 + [vmem] * 3,
        input_output_aliases={1: 3, 2: 4, 3: 5},
        scratch_shapes=[pltpu.SemaphoreType.DMA((3 * PIECES,))],
        compiler_params=pltpu.CompilerParams(vmem_limit_bytes=1 << 21),
        cost_estimate=pl.CostEstimate(flops=0, bytes_accessed=3 * dense_bytes, transcendentals=0),
        name="finish",
    )(ids, acc, mom, wts, kept, mrows, wrows)
    return new_weights, new_momentum, new_residual[None]


def solution(mesh):
    placed = (P("dp", None, None), P("dp", None, None), P(), P(), P(), P(), P(), P())
    return jax.shard_map(
        functools.partial(local, mesh.shape["dp"]),
        mesh=mesh,
        in_specs=placed,
        out_specs=(P(), P(), P("dp", None, None)),
        check_vma=False,
    )
```

time: 22 us -> 21.3 us (0.968)
  Pallas kernels: 21.2 us -> 20.5 us
    pallas_call x1, Pallas kernels: 18.1 us -> 17.3 us  [local(): pl.pallas_call(functools.partial(exchange, n, chunk), out_shape=(dense, d...]
where the time goes in v5:
time: 21.3 us; the launch traced here: 21.1 us
  Pallas kernels  20.5 us (96%)
  between operations  0.64 us (3%)
    pallas_call x1, Pallas kernels, local(): pl.pallas_call(functools.partial(exchange, n, chunk), out_shape=(dense, d...  17.3 us
    pallas_call x1, Pallas kernels, local(): pl.pallas_call(finish, out_shape=(whole, whole, whole, dense, dense, dens...  3.15 us

profile of v5, /device:TPU:0, one launch (start us, length us, event | category | flops | bytes accessed | tf_op | source)
XLA Modules:
  0.0 21.1 jit_solution(10469563649540500591)
XLA Ops:
  0.6 17.3 %exchange.1 = (f32[4096,128]{1,0:T(8,128)S(1)}, f32[4096,128]{1,0:T(8,128)S(1)}, f32[4096,128]{1,0:T(8,128)S(1)}, f32[32,8,128]{2,1,0:T(8,128)S(1)}, f32[32,8,12...) custom-call(f32[4096,128]{1,0:T(8,128)} %bitcast.5, f32[4096,128]{1,0:T(8,128)} %bitcast.6, ...), custom_call_target="tpu_custom_call" | custom-call | flops 2621440 | bytes 8388608 | tf_op jit(solution)/shard_map/exchange/pallas_call | solution.py:234
  18.0 3.2 %finish.1 = (f32[4096,128]{1,0:T(8,128)}, f32[4096,128]{1,0:T(8,128)}, f32[4096,128]{1,0:T(8,128)}, f32[4096,128]{1,0:T(8,128)S(1)}, f32[4096,128]{1,0:T(8,128)S(1)}, /*index=5*/f32[4096,128]{1,0:T(8,128)S(1)}) custom-call(s32[8,32]{1,0:T(8,128)S(4)} %get-tuple-element.13.ids, ...), custom_call_target="tpu_custom_call", output_to_operand_aliasing={{3}: (1, {}), {4}: (2, {}), {5}: (3, {})} | custom-call | bytes 6291456 | tf_op jit(solution)/shard_map/finish/pallas_call | solution.py:281

commit v6 on v5

--- a/solution.py
+++ b/solution.py
@@ -32,6 +32,7 @@
     outgoing, incoming, sender_blocks, updates,
     load_sem, table_sem, send_sems, recv_sems,
 ):
+    half = n // 2
     me = lax.axis_index("dp")
     cap, list_len = sel_s.shape[0], ids.shape[0]
     block_count, block_len = acc.shape
@@ -53,21 +54,28 @@
     for copy in tables[:4] + first_loads + tables[4:]:
         copy.start()
 
-    bits = [1 << i for i in range((n - 1).bit_length())]
-    my_bits = [(me // bit) % 2 for bit in bits]
-
-    def peer(step):
-        k = n - step
-        both = sum(mine * ((k // bit) % 2) * bit for mine, bit in zip(my_bits, bits))
-        return me + k - 2 * both
+    owner = me < half
+    share = 2 * me
+
+    def each_other(stop, act):
+        def step(device, _):
+            @pl.when(device != me)
+            def _():
+                act(device)
+            return 0
+
+        lax.fori_loop(0, stop, step, 0)
 
     barrier = pltpu.get_barrier_semaphore()
 
-    def greet(step, _):
-        pl.semaphore_signal(barrier, inc=1, device_id=(peer(step),), device_id_type=MESH)
-        return 0
-
-    lax.fori_loop(1, n, greet, 0)
+    def greet(device):
+        pl.semaphore_signal(barrier, inc=1, device_id=(device,), device_id_type=MESH)
+
+    each_other(half, greet)
+
+    @pl.when(owner)
+    def _():
+        lax.fori_loop(half, n, lambda device, _: (greet(device), 0)[1], 0)
 
     for copy in tables:
         copy.wait()
@@ -84,11 +92,15 @@
     flags_v[...] = jnp.where(slots < listed, hit, 0.0)
     flag_copy = pltpu.make_async_copy(flags_v, flags, table_sem.at[0])
     flag_copy.start()
-    lanes = lax.broadcasted_iota(jnp.int32, (n, cap, n), 2)
-    for_me = jnp.where(lanes == me, sel_v[...].astype(jnp.float32), 0.0)
-    sender_blocks[...] = jnp.broadcast_to(
-        jnp.sum(for_me, axis=2, keepdims=True), (n, cap, block_len)
-    )
+
+    @pl.when(owner)
+    def _():
+        lanes = lax.broadcasted_iota(jnp.int32, (n, cap, n), 2)
+        for side in range(2):
+            for_me = jnp.where(lanes == share + side, sel_v[...].astype(jnp.float32), 0.0)
+            sender_blocks[side] = jnp.broadcast_to(
+                jnp.sum(for_me, axis=2, keepdims=True), (n, cap, block_len)
+            )
 
     for copy in first_loads:
         copy.wait()
@@ -112,19 +124,23 @@
             device_id=(device,), device_id_type=MESH,
         )
 
-    def all_peers(buffer, phase):
-        part = buffer.at[pl.ds(0, n - 1)]
-        return remote(part, part, phase, peer(1))
-
-    pl.semaphore_wait(barrier, n - 1)
-
-    def send_to_owner(step, _):
-        o = peer(step)
-        remote(outgoing.at[o], incoming.at[me], 0, o).start()
-        return 0
-
-    lax.fori_loop(1, n, send_to_owner, 0)
-    incoming[me] = outgoing[me]
+    def arrived(part, phase):
+        return remote(part, part, phase, lax.rem(me + 1, n))
+
+    @pl.when(owner)
+    def _():
+        pl.semaphore_wait(barrier, n - 1)
+
+    @pl.when(jnp.logical_not(owner))
+    def _():
+        pl.semaphore_wait(barrier, half)
+
+    each_other(
+        half,
+        lambda device: remote(
+            outgoing.at[pl.ds(2 * device, 2)], incoming.at[me], 0, device
+        ).start(),
+    )
 
     def dense_acc(i, _):
         rows = pl.ds(pl.multiple_of(i * chunk, chunk), chunk)
@@ -132,18 +148,6 @@
         return 0
 
     lax.fori_loop(0, block_count // chunk, dense_acc, 0)
-    my_count = gcnt_s[me]
-    all_peers(incoming, 0).wait_recv()
-    for j in range(list_len):
-        block = jnp.where(j < my_count, ids[j, me], -1).astype(jnp.float32)
-        chosen = jnp.where(sender_blocks[...] == block, incoming[...], 0.0)
-        updates[me, pl.ds(j, 1), :] = jnp.sum(jnp.sum(chosen, axis=0), axis=0, keepdims=True)
-
-    def send_sum(step, _):
-        remote(updates.at[me], updates.at[me], 1, peer(step)).start()
-        return 0
-
-    lax.fori_loop(1, n, send_sum, 0)
     flag_copy.wait()
 
     def pick_kept(o, _):
@@ -174,12 +178,38 @@
         return 0
 
     lax.fori_loop(0, block_count // chunk, dense_step, 0)
-    all_peers(outgoing, 0).wait_send()
-    all_peers(updates, 1).wait_recv()
+
+    @pl.when(owner)
+    def _():
+        incoming[me] = outgoing[pl.ds(share, 2)]
+        arrived(incoming.at[pl.ds(0, n - 1)], 0).wait_recv()
+        for side in range(2):
+            listed_here = gcnt_s[share + side]
+            rows = incoming[:, side]
+            for j in range(list_len):
+                block = jnp.where(j < listed_here, ids[j, share + side], -1).astype(jnp.float32)
+                chosen = jnp.where(sender_blocks[side] == block, rows, 0.0)
+                updates[share + side, pl.ds(j, 1), :] = jnp.sum(
+                    jnp.sum(chosen, axis=0), axis=0, keepdims=True
+                )
+        own = updates.at[pl.ds(share, 2)]
+        each_other(n, lambda device: remote(own, own, 1, device).start())
+        arrived(outgoing.at[pl.ds(0, n - 2)], 0).wait_send()
+        arrived(updates.at[pl.ds(0, n - 2)], 1).wait_recv()
+
+    @pl.when(jnp.logical_not(owner))
+    def _():
+        arrived(outgoing, 0).wait_send()
+        arrived(updates, 1).wait_recv()
+
     new_rows = momentum_coef * mrows[...] + updates[...]
     mrows[...] = new_rows
     wrows[...] = wrows[...] - learning_rate * new_rows
-    all_peers(updates, 1).wait_send()
+
+    @pl.when(owner)
+    def _():
+        for _ in range(2):
+            arrived(updates.at[pl.ds(0, n - 1)], 1).wait_send()
 
 
 def finish(
@@ -248,8 +278,8 @@
             pltpu.VMEM((list_len, n), i32),
             pltpu.VMEM((list_len, n), f32),
             picks,
-            picks,
-            picks,
+            pltpu.VMEM((n, 2, cap, block_len), f32),
+            pltpu.VMEM((2, n, cap, block_len), f32),
             tiles,
             pltpu.SemaphoreType.DMA((4 * PIECES,)),
             pltpu.SemaphoreType.DMA((8,)),
@@ -258,7 +288,7 @@
         ],
         compiler_params=pltpu.CompilerParams(
             collective_id=0, has_side_effects=True,
-            vmem_limit_bytes=dense_bytes + 8 * tile_bytes + (1 << 21),
+            vmem_limit_bytes=dense_bytes + 12 * tile_bytes + (1 << 21),
         ),
         cost_estimate=pl.CostEstimate(
             flops=5 * block_count * block_len, bytes_accessed=4 * dense_bytes, transcendentals=0

time: 21.3 us -> 21.2 us (level)
  the two profiles are of different devices: /device:TPU:0 before, /device:TPU:31 now
where the time goes in v6:
time: 21.2 us; the launch traced here: 21 us
  Pallas kernels  20.3 us (96%)
  between operations  0.64 us (3%)
    pallas_call x1, Pallas kernels, local(): pl.pallas_call(functools.partial(exchange, n, chunk), out_shape=(dense, d...  17.2 us
    pallas_call x1, Pallas kernels, local(): pl.pallas_call(finish, out_shape=(whole, whole, whole, dense, dense, dens...  3.15 us

profile of v6, /device:TPU:31, one launch (start us, length us, event | category | flops | bytes accessed | tf_op | source)
XLA Modules:
  0.0 21.0 jit_solution(255687936845424656)
XLA Ops:
  0.6 17.2 %exchange.1 = (f32[4096,128]{1,0:T(8,128)S(1)}, f32[4096,128]{1,0:T(8,128)S(1)}, f32[4096,128]{1,0:T(8,128)S(1)}, f32[32,8,128]{2,1,0:T(8,128)S(1)}, f32[32,8,12...) custom-call(f32[4096,128]{1,0:T(8,128)} %bitcast.5, f32[4096,128]{1,0:T(8,128)} %bitcast.6, ...), custom_call_target="tpu_custom_call" | custom-call | flops 2621440 | bytes 8388608 | tf_op jit(solution)/shard_map/exchange/pallas_call | solution.py:264
  17.8 3.2 %finish.1 = (f32[4096,128]{1,0:T(8,128)}, f32[4096,128]{1,0:T(8,128)}, f32[4096,128]{1,0:T(8,128)}, f32[4096,128]{1,0:T(8,128)S(1)}, f32[4096,128]{1,0:T(8,128)S(1)}, /*index=5*/f32[4096,128]{1,0:T(8,128)S(1)}) custom-call(s32[8,32]{1,0:T(8,128)S(4)} %get-tuple-element.13.ids, ...), custom_call_target="tpu_custom_call", output_to_operand_aliasing={{3}: (1, {}), {4}: (2, {}), {5}: (3, {})} | custom-call | bytes 6291456 | tf_op jit(solution)/shard_map/finish/pallas_call | solution.py:311

commit v7 on v6

--- a/solution.py
+++ b/solution.py
@@ -55,7 +55,14 @@
         copy.start()
 
     owner = me < half
-    share = 2 * me
+    quarter = half // 2
+    core = me % 2
+    sibling = me + 1 - 2 * core
+
+    def share_of(device):
+        return 2 * ((device % 2) * quarter + device // 2)
+
+    share = share_of(me)
 
     def each_other(stop, act):
         def step(device, _):
@@ -76,6 +83,10 @@
     @pl.when(owner)
     def _():
         lax.fori_loop(half, n, lambda device, _: (greet(device), 0)[1], 0)
+
+    @pl.when(jnp.logical_not(owner))
+    def _():
+        greet(sibling)
 
     for copy in tables:
         copy.wait()
@@ -133,12 +144,12 @@
 
     @pl.when(jnp.logical_not(owner))
     def _():
-        pl.semaphore_wait(barrier, half)
+        pl.semaphore_wait(barrier, half + 1)
 
     each_other(
         half,
         lambda device: remote(
-            outgoing.at[pl.ds(2 * device, 2)], incoming.at[me], 0, device
+            outgoing.at[pl.ds(share_of(device), 2)], incoming.at[me], 0, device
         ).start(),
     )
 
@@ -193,14 +204,25 @@
                     jnp.sum(chosen, axis=0), axis=0, keepdims=True
                 )
         own = updates.at[pl.ds(share, 2)]
-        each_other(n, lambda device: remote(own, own, 1, device).start())
+        each_other(half, lambda device: remote(own, own, 1, device).start())
+
+        def send_up(i, _):
+            remote(own, own, 1, half + 2 * i + core).start()
+            return 0
+
+        lax.fori_loop(0, quarter, send_up, 0)
         arrived(outgoing.at[pl.ds(0, n - 2)], 0).wait_send()
         arrived(updates.at[pl.ds(0, n - 2)], 1).wait_recv()
 
     @pl.when(jnp.logical_not(owner))
     def _():
         arrived(outgoing, 0).wait_send()
-        arrived(updates, 1).wait_recv()
+        here, there = updates.at[pl.ds(core * half, half)], updates.at[pl.ds((1 - core) * half, half)]
+        arrived(here, 1).wait_recv()
+        relay = remote(here, here, 2, sibling)
+        relay.start()
+        relay.wait_send()
+        arrived(there, 2).wait_recv()
 
     new_rows = momentum_coef * mrows[...] + updates[...]
     mrows[...] = new_rows
@@ -208,8 +230,8 @@
 
     @pl.when(owner)
     def _():
-        for _ in range(2):
-            arrived(updates.at[pl.ds(0, n - 1)], 1).wait_send()
+        arrived(updates.at[pl.ds(0, n - 2)], 1).wait_send()
+        arrived(updates.at[pl.ds(0, half)], 1).wait_send()
 
 
 def finish(
@@ -283,8 +305,8 @@
             tiles,
             pltpu.SemaphoreType.DMA((4 * PIECES,)),
             pltpu.SemaphoreType.DMA((8,)),
-            pltpu.SemaphoreType.DMA((2,)),
-            pltpu.SemaphoreType.DMA((2,)),
+            pltpu.SemaphoreType.DMA((3,)),
+            pltpu.SemaphoreType.DMA((3,)),
         ],
         compiler_params=pltpu.CompilerParams(
             collective_id=0, has_side_effects=True,

time: 21.2 us -> 20.1 us (0.948)
  the two profiles are of different devices: /device:TPU:31 before, /device:TPU:25 now
where the time goes in v7:
time: 20.1 us; the launch traced here: 19.9 us
  Pallas kernels  19.3 us (96%)
  between operations  0.64 us (3%)
    pallas_call x1, Pallas kernels, local(): pl.pallas_call(functools.partial(exchange, n, chunk), out_shape=(dense, d...  16.1 us
    pallas_call x1, Pallas kernels, local(): pl.pallas_call(finish, out_shape=(whole, whole, whole, dense, dense, dens...  3.15 us

profile of v7, /device:TPU:25, one launch (start us, length us, event | category | flops | bytes accessed | tf_op | source)
XLA Modules:
  0.0 19.9 jit_solution(7381842844197360719)
XLA Ops:
  0.6 16.1 %exchange.1 = (f32[4096,128]{1,0:T(8,128)S(1)}, f32[4096,128]{1,0:T(8,128)S(1)}, f32[4096,128]{1,0:T(8,128)S(1)}, f32[32,8,128]{2,1,0:T(8,128)S(1)}, f32[32,8,12...) custom-call(f32[4096,128]{1,0:T(8,128)} %bitcast.5, f32[4096,128]{1,0:T(8,128)} %bitcast.6, ...), custom_call_target="tpu_custom_call" | custom-call | flops 2621440 | bytes 8388608 | tf_op jit(solution)/shard_map/exchange/pallas_call | solution.py:286
  16.7 3.2 %finish.1 = (f32[4096,128]{1,0:T(8,128)}, f32[4096,128]{1,0:T(8,128)}, f32[4096,128]{1,0:T(8,128)}, f32[4096,128]{1,0:T(8,128)S(1)}, f32[4096,128]{1,0:T(8,128)S(1)}, /*index=5*/f32[4096,128]{1,0:T(8,128)S(1)}) custom-call(s32[8,32]{1,0:T(8,128)S(4)} %get-tuple-element.13.ids, ...), custom_call_target="tpu_custom_call", output_to_operand_aliasing={{3}: (1, {}), {4}: (2, {}), {5}: (3, {})} | custom-call | bytes 6291456 | tf_op jit(solution)/shard_map/finish/pallas_call | solution.py:333

commit v8 on v7

--- a/solution.py
+++ b/solution.py
@@ -204,13 +204,13 @@
                     jnp.sum(chosen, axis=0), axis=0, keepdims=True
                 )
         own = updates.at[pl.ds(share, 2)]
+
+        def send_up(i, _):
+            remote(own, own, 1, n - 2 * i - 2 + core).start()
+            return 0
+
+        lax.fori_loop(0, quarter, send_up, 0)
         each_other(half, lambda device: remote(own, own, 1, device).start())
-
-        def send_up(i, _):
-            remote(own, own, 1, half + 2 * i + core).start()
-            return 0
-
-        lax.fori_loop(0, quarter, send_up, 0)
         arrived(outgoing.at[pl.ds(0, n - 2)], 0).wait_send()
         arrived(updates.at[pl.ds(0, n - 2)], 1).wait_recv()
 

time: 20.1 us -> 20 us (level)
  the two profiles are of different devices: /device:TPU:25 before, /device:TPU:17 now
where the time goes in v8:
time: 20 us; the launch traced here: 19.7 us
  Pallas kernels  19.1 us (96%)
  between operations  0.64 us (3%)
    pallas_call x1, Pallas kernels, local(): pl.pallas_call(functools.partial(exchange, n, chunk), out_shape=(dense, d...  16 us
    pallas_call x1, Pallas kernels, local(): pl.pallas_call(finish, out_shape=(whole, whole, whole, dense, dense, dens...  3.15 us

profile of v8, /device:TPU:17, one launch (start us, length us, event | category | flops | bytes accessed | tf_op | source)
XLA Modules:
  0.0 19.7 jit_solution(11004575662203912481)
XLA Ops:
  0.6 16.0 %exchange.1 = (f32[4096,128]{1,0:T(8,128)S(1)}, f32[4096,128]{1,0:T(8,128)S(1)}, f32[4096,128]{1,0:T(8,128)S(1)}, f32[32,8,128]{2,1,0:T(8,128)S(1)}, f32[32,8,12...) custom-call(f32[4096,128]{1,0:T(8,128)} %bitcast.5, f32[4096,128]{1,0:T(8,128)} %bitcast.6, ...), custom_call_target="tpu_custom_call" | custom-call | flops 2621440 | bytes 8388608 | tf_op jit(solution)/shard_map/exchange/pallas_call | solution.py:286
  16.6 3.2 %finish.1 = (f32[4096,128]{1,0:T(8,128)}, f32[4096,128]{1,0:T(8,128)}, f32[4096,128]{1,0:T(8,128)}, f32[4096,128]{1,0:T(8,128)S(1)}, f32[4096,128]{1,0:T(8,128)S(1)}, /*index=5*/f32[4096,128]{1,0:T(8,128)S(1)}) custom-call(s32[8,32]{1,0:T(8,128)S(4)} %get-tuple-element.13.ids, ...), custom_call_target="tpu_custom_call", output_to_operand_aliasing={{3}: (1, {}), {4}: (2, {}), {5}: (3, {})} | custom-call | bytes 6291456 | tf_op jit(solution)/shard_map/finish/pallas_call | solution.py:333

commit v9 on v8

--- a/solution.py
+++ b/solution.py
@@ -206,7 +206,7 @@
         own = updates.at[pl.ds(share, 2)]
 
         def send_up(i, _):
-            remote(own, own, 1, n - 2 * i - 2 + core).start()
+            remote(own, own, 1, half + 2 * ((i + me // 2) % quarter) + core).start()
             return 0
 
         lax.fori_loop(0, quarter, send_up, 0)

time: 20 us -> 19.8 us (0.990)
  the two profiles are of different devices: /device:TPU:17 before, /device:TPU:25 now
where the time goes in v9:
time: 19.8 us; the launch traced here: 19.5 us
  Pallas kernels  18.9 us (95%)
  between operations  0.64 us (3%)
    pallas_call x1, Pallas kernels, local(): pl.pallas_call(functools.partial(exchange, n, chunk), out_shape=(dense, d...  15.8 us
    pallas_call x1, Pallas kernels, local(): pl.pallas_call(finish, out_shape=(whole, whole, whole, dense, dense, dens...  3.15 us

profile of v9, /device:TPU:25, one launch (start us, length us, event | category | flops | bytes accessed | tf_op | source)
XLA Modules:
  0.0 19.5 jit_solution(1024603908058891093)
XLA Ops:
  0.6 15.8 %exchange.1 = (f32[4096,128]{1,0:T(8,128)S(1)}, f32[4096,128]{1,0:T(8,128)S(1)}, f32[4096,128]{1,0:T(8,128)S(1)}, f32[32,8,128]{2,1,0:T(8,128)S(1)}, f32[32,8,12...) custom-call(f32[4096,128]{1,0:T(8,128)} %bitcast.5, f32[4096,128]{1,0:T(8,128)} %bitcast.6, ...), custom_call_target="tpu_custom_call" | custom-call | flops 2621440 | bytes 8388608 | tf_op jit(solution)/shard_map/exchange/pallas_call | solution.py:286
  16.4 3.2 %finish.1 = (f32[4096,128]{1,0:T(8,128)}, f32[4096,128]{1,0:T(8,128)}, f32[4096,128]{1,0:T(8,128)}, f32[4096,128]{1,0:T(8,128)S(1)}, f32[4096,128]{1,0:T(8,128)S(1)}, /*index=5*/f32[4096,128]{1,0:T(8,128)S(1)}) custom-call(s32[8,32]{1,0:T(8,128)S(4)} %get-tuple-element.13.ids, ...), custom_call_target="tpu_custom_call", output_to_operand_aliasing={{3}: (1, {}), {4}: (2, {}), {5}: (3, {})} | custom-call | bytes 6291456 | tf_op jit(solution)/shard_map/finish/pallas_call | solution.py:333
